TPU v7x, 32 devices: a whole 2x2x4 slice. The times are simulated.
32 devices in a mesh: groups: 2 (over y), tm: 4 (over z), tile: 2 (over x), arrow: 2 (over core).
Axes of the slice: x: 2, y: 2, z: 4, core: 2. Of those that a mesh axis runs over, the one named last changes fastest.
Arguments:
- forward_blocks: float32 [8, 96, 1024], P(('groups', 'tm'), ('tile', 'arrow')), parts along dimension 0, may hold values from -3 to 3
- arrow_rhs: float32 [192, 64], P(('groups', 'tile', 'arrow')), parts along dimension 0, may hold values from -6 to 6
- diag_inverse: bfloat16 [8, 1024, 1024], P(('groups', 'tm'), None, ('tile', 'arrow')), parts along dimension 0
- lower_coupling: bfloat16 [8, 1024, 1024], P(('groups', 'tm'), None, ('tile', 'arrow')), parts along dimension 0
- arrow_slab: bfloat16 [8, 64, 1024], P(('groups', 'tm'), 'arrow'), parts along dimension 0, may hold values from -0.09375 to 0.09375
- arrow_inverse: float32 [128, 64], P('groups'), parts along dimension 0
- boundary_term: float32 [192, 1024], P(('groups', 'tile', 'arrow')), parts along dimension 0, may hold values from -6 to 6
Outputs:
- solution: float32 [8, 96, 1024], P(('groups', 'tm'), ('tile', 'arrow')), parts along dimension 0
- arrow_solution: float32 [192, 64], P(('groups', 'tile', 'arrow')), parts along dimension 0
There are 2 independent parts, one for each index of `groups`. A program takes and returns all parts, laid end to end along the dimension named above; each array names one. Nothing has to cross between parts.
All inputs are finite; a program needn't handle non-finite values.
Results may differ from a plain program's by a relative error of at most 0.007.
Values may be sent and summed in bfloat16 or wider, within the bound.
A program may use at most 64 MiB of HBM per device.

v0:
```python
import jax
import jax.numpy as jnp
from jax import lax
from jax.sharding import PartitionSpec as P


def from_behind(block, axis, distance):
    devices = range(lax.axis_size(axis))
    route = [(i - distance, i) for i in devices if i - distance in devices]
    return lax.ppermute(block, axis, route)


def shards(
    forward_blocks,
    arrow_rhs,
    diag_inverse,
    lower_coupling,
    arrow_slab,
    arrow_inverse,
    boundary_term,
):
    highest = lax.Precision.HIGHEST
    slab_full = lax.all_gather(arrow_slab, "arrow", axis=1, tiled=True)
    slab_wide = slab_full[0].astype(jnp.float32)
    block_rows = forward_blocks[0]
    local_part = jnp.dot(block_rows, slab_wide.T, precision=highest)
    arrow_sum = lax.psum(local_part, "tm")
    arrow_forward = jnp.dot(arrow_rhs - arrow_sum, arrow_inverse.T, precision=highest)
    arrow_solution = jnp.dot(arrow_forward, arrow_inverse, precision=highest)
    arrow_term = jnp.dot(arrow_solution, slab_wide, precision=highest)
    source_rows = block_rows - arrow_term
    inverse_full, lower_full = (
        lax.all_gather(diag_inverse, ("tile", "arrow"), axis=2, tiled=True),
        lax.all_gather(lower_coupling, ("tile", "arrow"), axis=2, tiled=True),
    )
    coupling = jnp.dot(inverse_full[0], lower_full[0], preferred_element_type=jnp.float32).astype(
        jnp.bfloat16
    )
    coupling_wide = coupling.astype(jnp.float32)
    is_last = (lax.axis_index("tm") == lax.axis_size("tm") - 1).astype(jnp.float32)
    entry_term = is_last * boundary_term

    def one_turn(turn_index, carry_in):
        residual = source_rows - carry_in
        outgoing = jnp.dot(residual, coupling_wide, precision=highest)
        return entry_term + from_behind(outgoing, "tm", -1)

    carry_in = lax.fori_loop(0, lax.axis_size("tm") - 1, one_turn, entry_term)
    residual = source_rows - carry_in
    solution = jnp.dot(
        residual.astype(jnp.bfloat16), inverse_full[0], preferred_element_type=jnp.float32
    )
    return (solution[None], arrow_solution)


def solution(mesh):
    return jax.shard_map(
        shards,
        mesh=mesh,
        in_specs=(
            P(("groups", "tm"), ("tile", "arrow"), None),
            P(("groups", "tile", "arrow"), None),
            P(("groups", "tm"), None, ("tile", "arrow")),
            P(("groups", "tm"), None, ("tile", "arrow")),
            P(("groups", "tm"), "arrow", None),
            P("groups", None),
            P(("groups", "tile", "arrow"), None),
        ),
        out_specs=(
            P(("groups", "tm"), ("tile", "arrow"), None),
            P(("groups", "tile", "arrow"), None),
        ),
        check_vma=False,
    )
```

profile of v0, /device:TPU:0, one launch (start us, length us, event | category | flops | bytes accessed | tf_op | source)
XLA Modules:
  0.0 106.9 jit_solution(2100586051761688842)
XLA Ops:
  7.2 0.0 copy-start
  7.2 0.0 copy-start.2
  7.2 0.0 all-gather.3.cloned.1.call-start
  7.2 0.7 all-gather.3.cloned.1.call-update
  7.9 0.0 all-gather.5.cloned.1.call-start
  8.0 0.7 all-gather.5.cloned.1.call-update
  8.7 0.9 broadcast_multiply_fusion
  9.6 2.2 %all_gather.9 = bf16[1,64,1024]{2,1,0:T(8,128)(2,1)S(1)} all-gather(bf16[1,32,1024]{2,1,0:T(8,128)(2,1)} %param.13), channel_id=1, replica_groups=mesh['groups'=2,'tm'=4,'tile'=2,'arrow'=2] {'arrow'}, dimensions={1}, use_global_device_ids=true | all-gather | bytes 196608 | tf_op jit(solution)/shard_map/all_gather | solution.py:23
  11.8 1.1 fusion.15
  12.9 20.3 %psum.7 = f32[24,64]{1,0:T(8,128)S(1)} all-reduce(f32[24,64]{1,0:T(8,128)S(1)} %fusion.15), channel_id=1, replica_groups=mesh['groups'=2,'tm'=4,'tile'=2,'arrow'=2] {'tm'}, use_global_device_ids=true, to_apply=%region_0.0 | all-reduce | flops 1536 | bytes 12288 | tf_op jit(solution)/shard_map/psum | solution.py:27
  33.2 0.0 copy-done
  33.2 0.9 fusion.18
  34.1 0.2 fusion.20
  34.2 0.0 copy-done.2
  34.3 0.0 copy-start.3
  34.3 0.2 convolution_subtract_fusion
  34.5 0.7 all-gather.3.cloned.1.call-done
  35.1 24.4 %all-gather.5.cloned.1.call-done = bf16[1,1024,1024]{2,1,0:T(8,128)(2,1)} async-done(((bf16[1,1024,256]{2,1,0:T(8,128)(2,1)}), bf16[1,1024,1024]{2,1,0:T(8,128)(2,1)}) %all-gather.5.cloned.1.call-update) | async-done | bytes 2097168 | tf_op jit(solution)/shard_map/all_gather | solution.py:34
  59.6 6.5 %convert_convert_fusion = f32[1024,1024]{1,0:T(8,128)} fusion(bf16[1,1024,1024]{2,1,0:T(8,128)(2,1)} %all-gather.5.cloned.1.call-done, bf16[1,1024,1024]{2,1,0:T(8,128)(2,1)} %all-gather.3.cloned.1.call-done), kind=kOutput, calls=%fused_computation.7 | convolution fusion | flops 2149580800 | bytes 8388608 | tf_op jit(solution)/shard_map/dot_general | solution.py:36
  66.1 0.0 copy-done.3
  66.1 0.0 copy-start.1
  66.1 32.9 %while.10 = (s32[]{:T(128)}, f32[24,1024]{1,0:T(8,128)S(1)}, f32[24,1024]{1,0:T(8,128)S(1)}, f32[1024,1024]{1,0:T(8,128)}, f32[24,1024]{1,0:T(8,128)S(1)}, /*index=5*/s32[]{:T(128)}) while((s32[]{:T(128)}, f32[24,1024]{1,0:T(8,128)S(1)}, f32[24,1024]{1,0:T(8,128)S(1)}, f32[1024,1024]{1,0:T(8,128)}, f32[24,1024]{1,0:T(8,128)S(1)}, ...), condition=%wide.region_2.0_spmd, body=%wide.region_1.0_spmd.sunk | while | flops 302039040 | bytes 5177453 | solution.py:48
  66.1 4.4 %fusion.31 = f32[24,1024]{1,0:T(8,128)S(1)} fusion(f32[1024,1024]{1,0:T(8,128)} %get-tuple-element.86, f32[24,1024]{1,0:T(8,128)S(1)} %get-tuple-element.85, f32[24,1024]{1,0:T(8,128)S(1)} %get-tuple-element.78), kind=kOutput, calls=%fused_computation.clone.1 | convolution fusion | flops 302014464 | bytes 4489216 | tf_op jit(solution)/shard_map/while/body/eval_jaxpr/dot_general | solution.py:45
  70.5 1.3 %collective-permute-start = (f32[24,1024]{1,0:T(8,128)S(1)}, f32[24,1024]{1,0:T(8,128)S(1)}, u32[]{:S(2)}, u32[]{:S(2)}) collective-permute-start(f32[24,1024]{1,0:T(8,128)S(1)} %fusion.31), channel_id=1, source_target_pairs={{4,0},{8,4},{12,8},{5,1},{9,5},{13,9},{6,2},{10,6},{14,10},{7,3},{... | collective-permute-start | bytes 294920 | tf_op jit(solution)/shard_map/while/body/eval_jaxpr/ppermute | solution.py:10
  71.8 5.6 %collective-permute-done = f32[24,1024]{1,0:T(8,128)S(1)} collective-permute-done((f32[24,1024]{1,0:T(8,128)S(1)}, f32[24,1024]{1,0:T(8,128)S(1)}, u32[]{:S(2)}, u32[]{:S(2)}) %collective-permute-start) | collective-permute-done | bytes 98336 | tf_op jit(solution)/shard_map/while/body/eval_jaxpr/ppermute | solution.py:10
  77.4 4.3 %fusion.31 = f32[24,1024]{1,0:T(8,128)S(1)} fusion(f32[1024,1024]{1,0:T(8,128)} %get-tuple-element.86, f32[24,1024]{1,0:T(8,128)S(1)} %get-tuple-element.85, f32[24,1024]{1,0:T(8,128)S(1)} %get-tuple-element.78), kind=kOutput, calls=%fused_computation.clone.1 | convolution fusion | flops 302014464 | bytes 4489216 | tf_op jit(solution)/shard_map/while/body/eval_jaxpr/dot_general | solution.py:45
  81.7 1.3 %collective-permute-start = (f32[24,1024]{1,0:T(8,128)S(1)}, f32[24,1024]{1,0:T(8,128)S(1)}, u32[]{:S(2)}, u32[]{:S(2)}) collective-permute-start(f32[24,1024]{1,0:T(8,128)S(1)} %fusion.31), channel_id=1, source_target_pairs={{4,0},{8,4},{12,8},{5,1},{9,5},{13,9},{6,2},{10,6},{14,10},{7,3},{... | collective-permute-start | bytes 294920 | tf_op jit(solution)/shard_map/while/body/eval_jaxpr/ppermute | solution.py:10
  83.0 5.2 %collective-permute-done = f32[24,1024]{1,0:T(8,128)S(1)} collective-permute-done((f32[24,1024]{1,0:T(8,128)S(1)}, f32[24,1024]{1,0:T(8,128)S(1)}, u32[]{:S(2)}, u32[]{:S(2)}) %collective-permute-start) | collective-permute-done | bytes 98336 | tf_op jit(solution)/shard_map/while/body/eval_jaxpr/ppermute | solution.py:10
  88.2 4.3 %fusion.31 = f32[24,1024]{1,0:T(8,128)S(1)} fusion(f32[1024,1024]{1,0:T(8,128)} %get-tuple-element.86, f32[24,1024]{1,0:T(8,128)S(1)} %get-tuple-element.85, f32[24,1024]{1,0:T(8,128)S(1)} %get-tuple-element.78), kind=kOutput, calls=%fused_computation.clone.1 | convolution fusion | flops 302014464 | bytes 4489216 | tf_op jit(solution)/shard_map/while/body/eval_jaxpr/dot_general | solution.py:45
  92.5 1.3 %collective-permute-start = (f32[24,1024]{1,0:T(8,128)S(1)}, f32[24,1024]{1,0:T(8,128)S(1)}, u32[]{:S(2)}, u32[]{:S(2)}) collective-permute-start(f32[24,1024]{1,0:T(8,128)S(1)} %fusion.31), channel_id=1, source_target_pairs={{4,0},{8,4},{12,8},{5,1},{9,5},{13,9},{6,2},{10,6},{14,10},{7,3},{... | collective-permute-start | bytes 294920 | tf_op jit(solution)/shard_map/while/body/eval_jaxpr/ppermute | solution.py:10
  93.8 5.2 %collective-permute-done = f32[24,1024]{1,0:T(8,128)S(1)} collective-permute-done((f32[24,1024]{1,0:T(8,128)S(1)}, f32[24,1024]{1,0:T(8,128)S(1)}, u32[]{:S(2)}, u32[]{:S(2)}) %collective-permute-start) | collective-permute-done | bytes 98336 | tf_op jit(solution)/shard_map/while/body/eval_jaxpr/ppermute | solution.py:10
  99.0 0.0 copy-done.1
  99.0 1.0 fusion.11
  (4 shorter events, 0.0 us)
Async XLA Ops:
  7.2 26.0 %copy-start = (f32[64,64]{1,0:T(8,128)S(1)}, f32[64,64]{1,0:T(8,128)}, u32[]{:S(2)}) copy-start(f32[64,64]{1,0:T(8,128)} %param.14) | copy-start | bytes 49156
  7.2 27.1 %copy-start.2 = (f32[1,24,1024]{2,1,0:T(8,128)S(1)}, f32[1,24,1024]{2,1,0:T(8,128)}, u32[]{:S(2)}) copy-start(f32[1,24,1024]{2,1,0:T(8,128)} %param.9) | copy-start | bytes 294916
  7.2 28.0 %all-gather.3.cloned.1.call-start = ((), (), s32[]{:S(2)}) async-start(), calls=%async_computation | async-start | bytes 2621440 | tf_op jit(solution)/shard_map/all_gather | solution.py:33
  7.9 51.6 %all-gather.5.cloned.1.call-start = ((), (), s32[]{:S(2)}) async-start(), calls=%async_computation.1 | async-start | bytes 2621440 | tf_op jit(solution)/shard_map/all_gather | solution.py:34
  34.3 31.8 %copy-start.3 = (f32[24,64]{1,0:T(8,128)}, f32[24,64]{1,0:T(8,128)S(1)}, u32[]{:S(2)}) copy-start(f32[24,64]{1,0:T(8,128)S(1)} %fusion.20) | copy-start | bytes 18436
  66.1 33.0 %copy-start.1 = (bf16[1,1024,1024]{2,1,0:T(8,128)(2,1)S(1)}, bf16[1,1024,1024]{2,1,0:T(8,128)(2,1)}, u32[]{:S(2)}) copy-start(bf16[1,1024,1024]{2,1,0:T(8,128)(2,1)} %all-gather.3.cloned.1.call-done) | copy-start | bytes 6291460
  70.5 6.8 %collective-permute-start = (f32[24,1024]{1,0:T(8,128)S(1)}, f32[24,1024]{1,0:T(8,128)S(1)}, u32[]{:S(2)}, u32[]{:S(2)}) collective-permute-start(f32[24,1024]{1,0:T(8,128)S(1)} %fusion.31), channel_id=1, source_target_pairs={{4,0},{8,4},{12,8},{5,1},{9,5},{13,9},{6,2},{10,6},{14,10},{7,3},{... | collective-permute-start | bytes 294920 | tf_op jit(solution)/shard_map/while/body/eval_jaxpr/ppermute | solution.py:10
  81.7 6.5 %collective-permute-start = (f32[24,1024]{1,0:T(8,128)S(1)}, f32[24,1024]{1,0:T(8,128)S(1)}, u32[]{:S(2)}, u32[]{:S(2)}) collective-permute-start(f32[24,1024]{1,0:T(8,128)S(1)} %fusion.31), channel_id=1, source_target_pairs={{4,0},{8,4},{12,8},{5,1},{9,5},{13,9},{6,2},{10,6},{14,10},{7,3},{... | collective-permute-start | bytes 294920 | tf_op jit(solution)/shard_map/while/body/eval_jaxpr/ppermute | solution.py:10
  92.5 6.5 %collective-permute-start = (f32[24,1024]{1,0:T(8,128)S(1)}, f32[24,1024]{1,0:T(8,128)S(1)}, u32[]{:S(2)}, u32[]{:S(2)}) collective-permute-start(f32[24,1024]{1,0:T(8,128)S(1)} %fusion.31), channel_id=1, source_target_pairs={{4,0},{8,4},{12,8},{5,1},{9,5},{13,9},{6,2},{10,6},{14,10},{7,3},{... | collective-permute-start | bytes 294920 | tf_op jit(solution)/shard_map/while/body/eval_jaxpr/ppermute | solution.py:10
Sparse Core Ops, SparseCore 0:
  9.6 25.5 all-gather.2
  36.7 22.8 all-gather.4
where the time goes:
time: 107 us
  waiting for transfers between devices  42.5 us (40%)
  matrix products  22.8 us (21%)
  blocking collectives  22.6 us (21%)
  between operations  14.1 us (13%)
  starting transfers between devices  3.94 us (4%)
    all_gather x1, waiting for transfers between devices, shards(): lax.all_gather(lower_coupling, ('tile', 'arrow'), axis=2, tiled=True)  24.4 us
    psum x1, blocking collectives, shards(): arrow_sum = lax.psum(local_part, 'tm')  20.3 us
    ppermute x3, waiting for transfers between devices, from_behind(): return lax.ppermute(block, axis, route)  16 us
    dot_general x3, matrix products, one_turn(): outgoing = jnp.dot(residual, coupling_wide, precision=highest)  13 us
    dot_general x1, matrix products, shards(): jnp.dot(inverse_full[0], lower_full[0], preferred_element_type=jnp.float32)  6.5 us
    ppermute x3, starting transfers between devices, from_behind(): return lax.ppermute(block, axis, route)  3.86 us
    all_gather x1, blocking collectives, shards(): slab_full = lax.all_gather(arrow_slab, 'arrow', axis=1, tiled=True)  2.21 us
  transfers between devices with their start and end apart: 5, of which 5 were waited for; matrix products, arithmetic and copies ran while one was open for 3% of the time, Pallas kernels for 0%

commit v1 on v0

--- a/solution.py
+++ b/solution.py
@@ -24,7 +24,11 @@
     slab_wide = slab_full[0].astype(jnp.float32)
     block_rows = forward_blocks[0]
     local_part = jnp.dot(block_rows, slab_wide.T, precision=highest)
-    arrow_sum = lax.psum(local_part, "tm")
+    arrow_sum = local_part
+    for hop in (1, 2):
+        arrow_sum = arrow_sum + lax.ppermute(
+            arrow_sum, "tm", [(dev, dev ^ hop) for dev in range(4)]
+        )
     arrow_forward = jnp.dot(arrow_rhs - arrow_sum, arrow_inverse.T, precision=highest)
     arrow_solution = jnp.dot(arrow_forward, arrow_inverse, precision=highest)
     arrow_term = jnp.dot(arrow_solution, slab_wide, precision=highest)

time: 107 us -> 107 us (level)
  blocking collectives: 22.6 us -> 2.21 us
  waiting for transfers between devices: 42.5 us -> 56.7 us
  starting transfers between devices: 3.94 us -> 9.95 us
    psum x1 -> x0, blocking collectives: 20.3 us -> none  [shards(): arrow_sum = lax.psum(local_part, 'tm')]
    all_gather x1, waiting for transfers between devices: 0.68 us -> 12.6 us  [shards(): lax.all_gather(diag_inverse, ('tile', 'arrow'), axis=2, tiled=True)]
    ppermute x0 -> x2, starting transfers between devices: none -> 6.01 us  [shards(): lax.ppermute(arrow_sum, 'tm', [(dev, dev ^ hop) for dev in range(4)])]
    ppermute x0 -> x2, waiting for transfers between devices: none -> 2.4 us  [shards(): lax.ppermute(arrow_sum, 'tm', [(dev, dev ^ hop) for dev in range(4)])]
  transfers between devices with their start and end apart: 5 -> 7, of which waited for: 5 -> 7; matrix products, arithmetic and copies ran while one was open for 3% -> 3% of each run, Pallas kernels for 0% -> 0%
where the time goes in v1:
time: 107 us
  waiting for transfers between devices  56.7 us (53%)
  matrix products  22.8 us (21%)
  between operations  14.1 us (13%)
  starting transfers between devices  9.95 us (9%)
  blocking collectives  2.21 us (2%)
    all_gather x1, waiting for transfers between devices, shards(): lax.all_gather(lower_coupling, ('tile', 'arrow'), axis=2, tiled=True)  24.4 us
    ppermute x3, waiting for transfers between devices, from_behind(): return lax.ppermute(block, axis, route)  16 us
    dot_general x3, matrix products, one_turn(): outgoing = jnp.dot(residual, coupling_wide, precision=highest)  13 us
    all_gather x1, waiting for transfers between devices, shards(): lax.all_gather(diag_inverse, ('tile', 'arrow'), axis=2, tiled=True)  12.6 us
    dot_general x1, matrix products, shards(): jnp.dot(inverse_full[0], lower_full[0], preferred_element_type=jnp.float32)  6.5 us
    ppermute x2, starting transfers between devices, shards(): lax.ppermute(arrow_sum, 'tm', [(dev, dev ^ hop) for dev in range(4)])  6.01 us
    ppermute x3, starting transfers between devices, from_behind(): return lax.ppermute(block, axis, route)  3.86 us
    ppermute x2, waiting for transfers between devices, shards(): lax.ppermute(arrow_sum, 'tm', [(dev, dev ^ hop) for dev in range(4)])  2.4 us
  transfers between devices with their start and end apart: 7, of which 7 were waited for; matrix products, arithmetic and copies ran while one was open for 3% of the time, Pallas kernels for 0%

profile of v1, /device:TPU:0, one launch (start us, length us, event | category | flops | bytes accessed | tf_op | source)
XLA Modules:
  0.0 106.9 jit_solution(15334228126374110423)
XLA Ops:
  7.2 0.0 copy-start
  7.2 0.0 copy-start.2
  7.2 0.0 all-gather.3.cloned.1.call-start
  7.2 0.7 all-gather.3.cloned.1.call-update
  7.9 0.0 all-gather.5.cloned.1.call-start
  8.0 0.7 all-gather.5.cloned.1.call-update
  8.7 2.2 %all_gather.9 = bf16[1,64,1024]{2,1,0:T(8,128)(2,1)S(1)} all-gather(bf16[1,32,1024]{2,1,0:T(8,128)(2,1)} %param.13), channel_id=1, replica_groups=mesh['groups'=2,'tm'=4,'tile'=2,'arrow'=2] {'arrow'}, dimensions={1}, use_global_device_ids=true | all-gather | bytes 196608 | tf_op jit(solution)/shard_map/all_gather | solution.py:23
  10.9 1.1 fusion.15
  11.9 3.0 %collective-permute-start.1 = (f32[24,64]{1,0:T(8,128)S(1)}, f32[24,64]{1,0:T(8,128)S(1)}, u32[]{:S(2)}, u32[]{:S(2)}) collective-permute-start(f32[24,64]{1,0:T(8,128)S(1)} %fusion.15), channel_id=1, source_target_pairs={{0,4},{4,0},{8,12},{12,8},{1,5},{5,1},{9,13},{13,9},{2,6},{6,2},{1... | collective-permute-start | bytes 18440 | tf_op jit(solution)/shard_map/ppermute | solution.py:29
  14.9 1.7 %collective-permute-done.1 = f32[24,64]{1,0:T(8,128)S(1)} collective-permute-done((f32[24,64]{1,0:T(8,128)S(1)}, f32[24,64]{1,0:T(8,128)S(1)}, u32[]{:S(2)}, u32[]{:S(2)}) %collective-permute-start.1) | collective-permute-done | bytes 6176 | tf_op jit(solution)/shard_map/ppermute | solution.py:29
  16.6 3.0 %collective-permute-start.2 = (f32[24,64]{1,0:T(8,128)S(1)}, f32[24,64]{1,0:T(8,128)S(1)}, u32[]{:S(2)}, u32[]{:S(2)}) collective-permute-start(f32[24,64]{1,0:T(8,128)S(1)} %add.12), channel_id=1, source_target_pairs={{0,8},{4,12},{8,0},{12,4},{1,9},{5,13},{9,1},{13,5},{2,10},{6,14},... | collective-permute-start | bytes 18440 | tf_op jit(solution)/shard_map/ppermute | solution.py:29
  19.6 0.9 broadcast_multiply_fusion
  20.6 0.7 collective-permute-done.2
  21.3 0.0 copy-done
  21.3 0.9 fusion.18
  22.2 0.1 fusion.21
  22.4 0.0 copy-done.2
  22.4 0.0 copy-start.3
  22.4 0.2 convolution_subtract_fusion
  22.6 12.6 %all-gather.3.cloned.1.call-done = bf16[1,1024,1024]{2,1,0:T(8,128)(2,1)} async-done(((bf16[1,1024,256]{2,1,0:T(8,128)(2,1)}), bf16[1,1024,1024]{2,1,0:T(8,128)(2,1)}) %all-gather.3.cloned.1.call-update) | async-done | bytes 2097168 | tf_op jit(solution)/shard_map/all_gather | solution.py:37
  35.1 24.4 %all-gather.5.cloned.1.call-done = bf16[1,1024,1024]{2,1,0:T(8,128)(2,1)} async-done(((bf16[1,1024,256]{2,1,0:T(8,128)(2,1)}), bf16[1,1024,1024]{2,1,0:T(8,128)(2,1)}) %all-gather.5.cloned.1.call-update) | async-done | bytes 2097168 | tf_op jit(solution)/shard_map/all_gather | solution.py:38
  59.6 6.5 %convert_convert_fusion = f32[1024,1024]{1,0:T(8,128)} fusion(bf16[1,1024,1024]{2,1,0:T(8,128)(2,1)} %all-gather.5.cloned.1.call-done, bf16[1,1024,1024]{2,1,0:T(8,128)(2,1)} %all-gather.3.cloned.1.call-done), kind=kOutput, calls=%fused_computation.7 | convolution fusion | flops 2149580800 | bytes 8388608 | tf_op jit(solution)/shard_map/dot_general | solution.py:40
  66.1 0.0 copy-done.3
  66.1 0.0 copy-start.1
  66.1 32.9 %while.10 = (s32[]{:T(128)}, f32[24,1024]{1,0:T(8,128)S(1)}, f32[24,1024]{1,0:T(8,128)S(1)}, f32[1024,1024]{1,0:T(8,128)}, f32[24,1024]{1,0:T(8,128)S(1)}, /*index=5*/s32[]{:T(128)}) while((s32[]{:T(128)}, f32[24,1024]{1,0:T(8,128)S(1)}, f32[24,1024]{1,0:T(8,128)S(1)}, f32[1024,1024]{1,0:T(8,128)}, f32[24,1024]{1,0:T(8,128)S(1)}, ...), condition=%wide.region_1.0_spmd, body=%wide.region_0.0_spmd.sunk | while | flops 302039040 | bytes 5177453 | solution.py:52
  66.1 4.4 %fusion.32 = f32[24,1024]{1,0:T(8,128)S(1)} fusion(f32[1024,1024]{1,0:T(8,128)} %get-tuple-element.86, f32[24,1024]{1,0:T(8,128)S(1)} %get-tuple-element.85, f32[24,1024]{1,0:T(8,128)S(1)} %get-tuple-element.78), kind=kOutput, calls=%fused_computation.clone.1 | convolution fusion | flops 302014464 | bytes 4489216 | tf_op jit(solution)/shard_map/while/body/eval_jaxpr/dot_general | solution.py:49
  70.5 1.3 %collective-permute-start = (f32[24,1024]{1,0:T(8,128)S(1)}, f32[24,1024]{1,0:T(8,128)S(1)}, u32[]{:S(2)}, u32[]{:S(2)}) collective-permute-start(f32[24,1024]{1,0:T(8,128)S(1)} %fusion.32), channel_id=1, source_target_pairs={{4,0},{8,4},{12,8},{5,1},{9,5},{13,9},{6,2},{10,6},{14,10},{7,3},{... | collective-permute-start | bytes 294920 | tf_op jit(solution)/shard_map/while/body/eval_jaxpr/ppermute | solution.py:10
  71.8 5.6 %collective-permute-done = f32[24,1024]{1,0:T(8,128)S(1)} collective-permute-done((f32[24,1024]{1,0:T(8,128)S(1)}, f32[24,1024]{1,0:T(8,128)S(1)}, u32[]{:S(2)}, u32[]{:S(2)}) %collective-permute-start) | collective-permute-done | bytes 98336 | tf_op jit(solution)/shard_map/while/body/eval_jaxpr/ppermute | solution.py:10
  77.4 4.3 %fusion.32 = f32[24,1024]{1,0:T(8,128)S(1)} fusion(f32[1024,1024]{1,0:T(8,128)} %get-tuple-element.86, f32[24,1024]{1,0:T(8,128)S(1)} %get-tuple-element.85, f32[24,1024]{1,0:T(8,128)S(1)} %get-tuple-element.78), kind=kOutput, calls=%fused_computation.clone.1 | convolution fusion | flops 302014464 | bytes 4489216 | tf_op jit(solution)/shard_map/while/body/eval_jaxpr/dot_general | solution.py:49
  81.7 1.3 %collective-permute-start = (f32[24,1024]{1,0:T(8,128)S(1)}, f32[24,1024]{1,0:T(8,128)S(1)}, u32[]{:S(2)}, u32[]{:S(2)}) collective-permute-start(f32[24,1024]{1,0:T(8,128)S(1)} %fusion.32), channel_id=1, source_target_pairs={{4,0},{8,4},{12,8},{5,1},{9,5},{13,9},{6,2},{10,6},{14,10},{7,3},{... | collective-permute-start | bytes 294920 | tf_op jit(solution)/shard_map/while/body/eval_jaxpr/ppermute | solution.py:10
  83.0 5.2 %collective-permute-done = f32[24,1024]{1,0:T(8,128)S(1)} collective-permute-done((f32[24,1024]{1,0:T(8,128)S(1)}, f32[24,1024]{1,0:T(8,128)S(1)}, u32[]{:S(2)}, u32[]{:S(2)}) %collective-permute-start) | collective-permute-done | bytes 98336 | tf_op jit(solution)/shard_map/while/body/eval_jaxpr/ppermute | solution.py:10
  88.2 4.3 %fusion.32 = f32[24,1024]{1,0:T(8,128)S(1)} fusion(f32[1024,1024]{1,0:T(8,128)} %get-tuple-element.86, f32[24,1024]{1,0:T(8,128)S(1)} %get-tuple-element.85, f32[24,1024]{1,0:T(8,128)S(1)} %get-tuple-element.78), kind=kOutput, calls=%fused_computation.clone.1 | convolution fusion | flops 302014464 | bytes 4489216 | tf_op jit(solution)/shard_map/while/body/eval_jaxpr/dot_general | solution.py:49
  92.5 1.3 %collective-permute-start = (f32[24,1024]{1,0:T(8,128)S(1)}, f32[24,1024]{1,0:T(8,128)S(1)}, u32[]{:S(2)}, u32[]{:S(2)}) collective-permute-start(f32[24,1024]{1,0:T(8,128)S(1)} %fusion.32), channel_id=1, source_target_pairs={{4,0},{8,4},{12,8},{5,1},{9,5},{13,9},{6,2},{10,6},{14,10},{7,3},{... | collective-permute-start | bytes 294920 | tf_op jit(solution)/shard_map/while/body/eval_jaxpr/ppermute | solution.py:10
  93.8 5.2 %collective-permute-done = f32[24,1024]{1,0:T(8,128)S(1)} collective-permute-done((f32[24,1024]{1,0:T(8,128)S(1)}, f32[24,1024]{1,0:T(8,128)S(1)}, u32[]{:S(2)}, u32[]{:S(2)}) %collective-permute-start) | collective-permute-done | bytes 98336 | tf_op jit(solution)/shard_map/while/body/eval_jaxpr/ppermute | solution.py:10
  99.0 0.0 copy-done.1
  99.0 1.0 fusion.11
  (5 shorter events, 0.0 us)
Async XLA Ops:
  7.2 14.2 %copy-start = (f32[64,64]{1,0:T(8,128)S(1)}, f32[64,64]{1,0:T(8,128)}, u32[]{:S(2)}) copy-start(f32[64,64]{1,0:T(8,128)} %param.14) | copy-start | bytes 49156
  7.2 15.2 %copy-start.2 = (f32[1,24,1024]{2,1,0:T(8,128)S(1)}, f32[1,24,1024]{2,1,0:T(8,128)}, u32[]{:S(2)}) copy-start(f32[1,24,1024]{2,1,0:T(8,128)} %param.9) | copy-start | bytes 294916
  7.2 28.0 %all-gather.3.cloned.1.call-start = ((), (), s32[]{:S(2)}) async-start(), calls=%async_computation | async-start | bytes 2621440 | tf_op jit(solution)/shard_map/all_gather | solution.py:37
  7.9 51.6 %all-gather.5.cloned.1.call-start = ((), (), s32[]{:S(2)}) async-start(), calls=%async_computation.1 | async-start | bytes 2621440 | tf_op jit(solution)/shard_map/all_gather | solution.py:38
  11.9 4.7 %collective-permute-start.1 = (f32[24,64]{1,0:T(8,128)S(1)}, f32[24,64]{1,0:T(8,128)S(1)}, u32[]{:S(2)}, u32[]{:S(2)}) collective-permute-start(f32[24,64]{1,0:T(8,128)S(1)} %fusion.15), channel_id=1, source_target_pairs={{0,4},{4,0},{8,12},{12,8},{1,5},{5,1},{9,13},{13,9},{2,6},{6,2},{1... | collective-permute-start | bytes 18440 | tf_op jit(solution)/shard_map/ppermute | solution.py:29
  16.6 4.7 %collective-permute-start.2 = (f32[24,64]{1,0:T(8,128)S(1)}, f32[24,64]{1,0:T(8,128)S(1)}, u32[]{:S(2)}, u32[]{:S(2)}) collective-permute-start(f32[24,64]{1,0:T(8,128)S(1)} %add.12), channel_id=1, source_target_pairs={{0,8},{4,12},{8,0},{12,4},{1,9},{5,13},{9,1},{13,5},{2,10},{6,14},... | collective-permute-start | bytes 18440 | tf_op jit(solution)/shard_map/ppermute | solution.py:29
  22.4 43.7 %copy-start.3 = (f32[24,64]{1,0:T(8,128)}, f32[24,64]{1,0:T(8,128)S(1)}, u32[]{:S(2)}) copy-start(f32[24,64]{1,0:T(8,128)S(1)} %fusion.21) | copy-start | bytes 18436
  66.1 33.0 %copy-start.1 = (bf16[1,1024,1024]{2,1,0:T(8,128)(2,1)S(1)}, bf16[1,1024,1024]{2,1,0:T(8,128)(2,1)}, u32[]{:S(2)}) copy-start(bf16[1,1024,1024]{2,1,0:T(8,128)(2,1)} %all-gather.3.cloned.1.call-done) | copy-start | bytes 6291460
  70.5 6.8 %collective-permute-start = (f32[24,1024]{1,0:T(8,128)S(1)}, f32[24,1024]{1,0:T(8,128)S(1)}, u32[]{:S(2)}, u32[]{:S(2)}) collective-permute-start(f32[24,1024]{1,0:T(8,128)S(1)} %fusion.32), channel_id=1, source_target_pairs={{4,0},{8,4},{12,8},{5,1},{9,5},{13,9},{6,2},{10,6},{14,10},{7,3},{... | collective-permute-start | bytes 294920 | tf_op jit(solution)/shard_map/while/body/eval_jaxpr/ppermute | solution.py:10
  81.7 6.5 %collective-permute-start = (f32[24,1024]{1,0:T(8,128)S(1)}, f32[24,1024]{1,0:T(8,128)S(1)}, u32[]{:S(2)}, u32[]{:S(2)}) collective-permute-start(f32[24,1024]{1,0:T(8,128)S(1)} %fusion.32), channel_id=1, source_target_pairs={{4,0},{8,4},{12,8},{5,1},{9,5},{13,9},{6,2},{10,6},{14,10},{7,3},{... | collective-permute-start | bytes 294920 | tf_op jit(solution)/shard_map/while/body/eval_jaxpr/ppermute | solution.py:10
  92.5 6.5 %collective-permute-start = (f32[24,1024]{1,0:T(8,128)S(1)}, f32[24,1024]{1,0:T(8,128)S(1)}, u32[]{:S(2)}, u32[]{:S(2)}) collective-permute-start(f32[24,1024]{1,0:T(8,128)S(1)} %fusion.32), channel_id=1, source_target_pairs={{4,0},{8,4},{12,8},{5,1},{9,5},{13,9},{6,2},{10,6},{14,10},{7,3},{... | collective-permute-start | bytes 294920 | tf_op jit(solution)/shard_map/while/body/eval_jaxpr/ppermute | solution.py:10
Sparse Core Ops, SparseCore 0:
  9.6 25.5 all-gather.2
  36.7 22.8 all-gather.4
